TPU v7x, 512 devices: a whole 4x8x8 slice. The times are simulated.
512 devices in a mesh: row: 32 (over x, y), inner: 16 (over z, core).
Axes of the slice: x: 4, y: 8, z: 8, core: 2. Of those that a mesh axis runs over, the one named last changes fastest.
Arguments:
- h_blocks: bfloat16 [512, 32, 128, 128], P('row', 'inner'), may hold values from -0.09375 to 0.09375
- block_cols: int32 [512, 32], P('row', 'inner'), may hold values from 0 to 511, as said below
- panel_now: bfloat16 [65536, 192], P(('row', 'inner')), may hold values from -6 to 6
- panel_prev: bfloat16 [65536, 192], P(('row', 'inner')), may hold values from -6 to 6
- density: float32 [65536, 192], P(('row', 'inner')), may hold values from -6 to 6
- coeff: float32 [1], replicated, may hold values from 0.5 to 2
- cot_panel: bfloat16 [65536, 192], P(('row', 'inner')), may hold values from -2 to 2
- cot_density: bfloat16 [65536, 192], P(('row', 'inner')), may hold values from -2 to 2
Outputs:
- panel_next: bfloat16 [65536, 192], P(('row', 'inner'))
- density_next: float32 [65536, 192], P(('row', 'inner'))
- grad_now: float32 [65536, 192], P(('row', 'inner'))
- grad_h: bfloat16 [512, 32, 128, 128], P('row', 'inner')
Inputs may be any that keep to these rules, and one draw needn't show every extreme that they name: `block_cols`: each block row b lists 32 distinct block columns, each within periodic distance 16 of b modulo 512.
All inputs are finite; a program needn't handle non-finite values.
Results may differ from a plain program's by a relative error of at most 0.022.
Values may be sent and summed in bfloat16 or wider, within the bound.
A program may use at most 64 MiB of HBM per device.

v0:
```python
import jax
import jax.numpy as jnp
from jax import lax
from jax.sharding import PartitionSpec as P


def with_halo(array, sides, width):
    for axis, dim in sides:
        devices, length = (lax.axis_size(axis), array.shape[dim])
        up = [(i, (i + 1) % devices) for i in range(devices)]
        down = [(j, i) for i, j in up]
        last = lax.slice_in_dim(array, length - width, length, axis=dim)
        first = lax.slice_in_dim(array, 0, width, axis=dim)
        before = lax.ppermute(last, axis, up)
        after = lax.ppermute(first, axis, down)
        array = jnp.concatenate([before, array, after], axis=dim)
    return array


def per_device(h_blocks, block_cols, panel_now, panel_prev, density, coeff, cot_panel, cot_density):
    rows_here, slots_here, block_size, _ = h_blocks.shape
    shard_rows, probe_count = panel_now.shape
    group_rows = rows_here * block_size
    inner_count = lax.axis_size("inner")
    block_total = rows_here * lax.axis_size("row")
    first_block = lax.axis_index("row") * rows_here
    group_panel = lax.all_gather(panel_now, "inner", axis=0, tiled=True)
    window = with_halo(group_panel, (("row", 0),), group_rows)
    window = window.reshape(3 * rows_here, block_size, probe_count)
    local_index = (block_cols - first_block + rows_here) % block_total
    picked = jnp.take(window, local_index, axis=0)
    partial_term = jnp.einsum(
        "rsij,rsjn->rin", h_blocks, picked, preferred_element_type=jnp.float32
    )
    product = lax.psum_scatter(
        partial_term.reshape(shard_rows * lax.axis_size("inner"), probe_count).astype(jnp.bfloat16),
        "inner",
        scatter_dimension=0,
        tiled=True,
    ).astype(jnp.float32)
    scale = coeff[0]
    panel_next = (2.0 * product - panel_prev.astype(jnp.float32)).astype(jnp.bfloat16)
    density_next = density + scale * panel_next.astype(jnp.float32)
    cot_total = (cot_panel.astype(jnp.float32) + scale * cot_density.astype(jnp.float32)).astype(
        jnp.bfloat16
    )
    cot_group = lax.all_gather(cot_total, "inner", axis=0, tiled=True)
    cot_group = cot_group.reshape(rows_here, block_size, probe_count)
    grad_h = (
        2.0 * jnp.einsum("rin,rsjn->rsij", cot_group, picked, preferred_element_type=jnp.float32)
    ).astype(jnp.bfloat16)
    targets = lax.broadcasted_iota(jnp.int32, (1, 3 * rows_here), 1)
    returned = jnp.zeros((3 * rows_here, block_size, probe_count), jnp.float32)
    for slot_index in range(slots_here):
        selector = (local_index[:, slot_index][:, None] == targets).astype(jnp.float32)
        back_slot = jnp.einsum(
            "rij,rin->rjn", h_blocks[:, slot_index], cot_group, preferred_element_type=jnp.float32
        )
        returned = returned + jnp.einsum(
            "rw,rjn->wjn", selector, back_slot, precision=lax.Precision.HIGHEST
        )
    term = returned.astype(jnp.bfloat16).reshape(3 * group_rows, probe_count)
    rimmed = with_halo(term, (("row", 0),), group_rows)
    stacked = jnp.stack(
        (rimmed[:group_rows], rimmed[2 * group_rows : 3 * group_rows], rimmed[4 * group_rows :]), 0
    )
    stacked = stacked.reshape(3, inner_count, shard_rows, probe_count)
    stacked = lax.all_to_all(stacked, "inner", split_axis=1, concat_axis=1, tiled=True)
    back = jnp.sum(stacked.astype(jnp.float32), axis=1).astype(jnp.bfloat16)
    total = jnp.sum(back.astype(jnp.float32), axis=0)
    grad_now = 2.0 * total
    return (panel_next, density_next, grad_now, grad_h)


def solution(mesh):
    in_specs = (
        P("row", "inner", None, None),
        P("row", "inner"),
        P(("row", "inner"), None),
        P(("row", "inner"), None),
        P(("row", "inner"), None),
        P(),
        P(("row", "inner"), None),
        P(("row", "inner"), None),
    )
    out_specs = (
        P(("row", "inner"), None),
        P(("row", "inner"), None),
        P(("row", "inner"), None),
        P("row", "inner", None, None),
    )
    return jax.shard_map(
        per_device, mesh=mesh, in_specs=in_specs, out_specs=out_specs, check_vma=False
    )
```

profile of v0, /device:TPU:1, one launch (start us, length us, event | category | flops | bytes accessed | tf_op | source)
XLA Modules:
  0.0 252.6 jit_solution(3069184094955324178)
XLA Ops:
  7.9 0.8 add_convert_fusion.1
  8.8 26.7 %all_gather.7 = bf16[2048,192]{0,1:T(8,128)(2,1)S(1)} all-gather(bf16[128,192]{0,1:T(8,128)(2,1)S(1)} %add_convert_fusion.1), channel_id=1, replica_groups=mesh['row'=32,'inner'=16] {'inner'}, dimensions={0}, use_global_device_ids=true | all-gather | bytes 835584 | tf_op jit(solution)/shard_map/all_gather | solution.py:47
  35.4 1.4 convolution_bitcast_fusion.1
  36.8 1.5 convolution_bitcast_fusion
  38.4 2.7 %fusion.1 = f32[48,128,192]{1,0,2:T(8,128)S(1)} fusion(f32[16,128,192]{1,2,0:T(8,128)S(1)} %convolution_bitcast_fusion.1, s32[16]{0:T(128)S(1)} %get-tuple-element.28), kind=kOutput, calls=%fused_computation.8 | convolution fusion | flops 226493184 | bytes 6291520 | tf_op jit(solution)/shard_map/rw,rjn->wjn/dot_general | solution.py:59
  41.1 3.8 %add_convert_fusion = bf16[48,128,192]{1,0,2:T(8,128)(2,1)S(1)} fusion(f32[48,128,192]{1,0,2:T(8,128)S(1)} %fusion.1, f32[16,128,192]{1,2,0:T(8,128)S(1)} %copy-done, s32[16]{0:T(128)S(1)} %get-tuple-element.27), kind=kOutput, calls=%fused_computation.1 | convolution fusion | flops 228852480 | bytes 8650816 | tf_op jit(solution)/shard_map/rw,rjn->wjn/dot_general | solution.py:59
  45.0 0.4 fusion.25
  45.4 0.2 copy.83
  45.6 3.2 %collective-permute-start.2 = (bf16[2048,192]{0,1:T(8,128)(2,1)S(1)}, bf16[2048,192]{0,1:T(8,128)(2,1)S(1)}, u32[]{:S(2)}, u32[]{:S(2)}) collective-permute-start(bf16[2048,192]{0,1:T(8,128)(2,1)S(1)} %bitcast.95), channel_id=1, source_target_pairs={{0,16},{16,32},{32,48},{48,64},{64,80},{80,96},{96,112},{112,128},... | collective-permute-start | bytes 2359304 | tf_op jit(solution)/shard_map/ppermute | solution.py:14
  48.8 0.2 copy.82
  49.0 6.0 %collective-permute-start.3 = (bf16[2048,192]{0,1:T(8,128)(2,1)S(1)}, bf16[2048,192]{0,1:T(8,128)(2,1)S(1)}, u32[]{:S(2)}, u32[]{:S(2)}) collective-permute-start(bf16[2048,192]{0,1:T(8,128)(2,1)S(1)} %bitcast.97), channel_id=1, source_target_pairs={{16,0},{32,16},{48,32},{64,48},{80,64},{96,80},{112,96},{128,112},... | collective-permute-start | bytes 2359304 | tf_op jit(solution)/shard_map/ppermute | solution.py:15
  55.0 15.6 %collective-permute-done.2 = bf16[2048,192]{0,1:T(8,128)(2,1)S(1)} collective-permute-done((bf16[2048,192]{0,1:T(8,128)(2,1)S(1)}, bf16[2048,192]{0,1:T(8,128)(2,1)S(1)}, u32[]{:S(2)}, u32[]{:S(2)}) %collective-permute-start.2) | collective-permute-done | bytes 786464 | tf_op jit(solution)/shard_map/ppermute | solution.py:14
  70.8 1.0 collective-permute-done.3
  72.0 0.3 pad_maximum_fusion
  72.2 2.0 copy.43
  74.3 4.6 %all-to-all-start = ((bf16[3,16,128,192]{2,3,0,1:T(8,128)(2,1)}), bf16[3,16,128,192]{2,3,0,1:T(8,128)(2,1)S(1)}, u32[]{:S(2)}, u32[]{:S(2)}) async-start(bf16[3,16,128,192]{2,3,0,1:T(8,128)(2,1)} %copy.43), calls=%async_computation | async-start | bytes 4718592 | tf_op jit(solution)/shard_map/all_to_all | solution.py:68
  78.9 69.1 %all_gather.6 = bf16[2048,192]{0,1:T(8,128)(2,1)} all-gather(bf16[128,192]{0,1:T(8,128)(2,1)S(1)} %copy-done.3), channel_id=1, replica_groups=mesh['row'=32,'inner'=16] {'inner'}, dimensions={0}, use_global_device_ids=true | all-gather | bytes 835584 | tf_op jit(solution)/shard_map/all_gather | solution.py:27
  148.0 1.9 collective-permute-start
  149.9 7.6 %collective-permute-start.1 = (bf16[2048,192]{0,1:T(8,128)(2,1)}, bf16[2048,192]{0,1:T(8,128)(2,1)}, u32[]{:S(2)}, u32[]{:S(2)}) collective-permute-start(bf16[2048,192]{0,1:T(8,128)(2,1)} %all_gather.6), channel_id=1, source_target_pairs={{16,0},{32,16},{48,32},{64,48},{80,64},{96,80},{112,96},{128,112},... | collective-permute-start | bytes 2359304 | tf_op jit(solution)/shard_map/ppermute | solution.py:15
  157.8 15.7 %collective-permute-done = bf16[2048,192]{0,1:T(8,128)(2,1)} collective-permute-done((bf16[2048,192]{0,1:T(8,128)(2,1)}, bf16[2048,192]{0,1:T(8,128)(2,1)}, u32[]{:S(2)}, u32[]{:S(2)}) %collective-permute-start) | collective-permute-done | bytes 786464 | tf_op jit(solution)/shard_map/ppermute | solution.py:14
  173.5 1.0 collective-permute-done.1
  174.5 3.7 %copy_bitcast_fusion = bf16[48,128,192]{1,2,0:T(8,128)(2,1)} fusion(bf16[2048,192]{0,1:T(8,128)(2,1)} %collective-permute-done.1, bf16[2048,192]{0,1:T(8,128)(2,1)} %all_gather.6, bf16[2048,192]{0,1:T(8,128)(2,1)} %collective-permute-done), kind=kLoop, calls=%fused_computation.2 | loop fusion | flops 7077888 | bytes 4718592 | tf_op jit(solution)/shard_map/reshape | solution.py:29
  178.1 3.6 %gather_fusion = bf16[32,128,192]{1,2,0:T(8,128)(2,1)} fusion(bf16[48,128,192]{1,2,0:T(8,128)(2,1)} %copy_bitcast_fusion, s32[1024]{0:T(1024)S(1)} %pad_clamp_fusion), kind=kCustom, calls=%fused_computation | custom fusion | bytes 3145856 | tf_op jit(solution)/shard_map/jit(_take)/gather | solution.py:31
  181.7 3.2 %fusion.4 = bf16[16,128,192]{1,2,0:T(8,128)(2,1)} fusion(bf16[16,2,128,128]{3,2,1,0:T(8,128)(2,1)} %param.8, bf16[16,2,128,192]{2,3,1,0:T(8,128)(2,1)} %bitcast.93, pred[16,2]{1,0:T(8,128)(4,1)S(1)} %copy.33), kind=kOutput, calls=%fused_computation.14 | convolution fusion | flops 202506240 | bytes 3407904 | tf_op jit(solution)/shard_map/rsij,rsjn->rin/dot_general | solution.py:32
  184.9 2.2 copy.53
  187.3 3.3 %fusion.3 = bf16[16,2,128,128]{2,3,1,0:T(8,128)(2,1)} fusion(bf16[16,2,128,192]{2,3,1,0:T(8,128)(2,1)} %bitcast.94, pred[16,2]{1,0:T(8,128)(4,1)S(1)} %copy.33, bf16[16,128,192,1]{1,0,2,3:T(8,128)(2,1)S(1)} %bitcast.99), kind=kOutput, calls=%fused_computation.13 | convolution fusion | flops 203161600 | bytes 3407904 | tf_op jit(solution)/shard_map/rin,rsjn->rsij/dot_general | solution.py:50
  190.6 2.3 copy.46
  192.9 50.1 %reduce-scatter.4.cloned.1.call-done = bf16[128,192]{1,0:T(8,128)(2,1)} async-done(((bf16[2048,192]{1,0:T(8,128)(2,1)}), bf16[128,192]{1,0:T(8,128)(2,1)}) %reduce-scatter.4.cloned.1.call-update) | async-done | bytes 49168
  243.0 0.9 copy.52
  244.0 0.7 multiply_add_fusion
  244.7 0.4 reduce_sum.21
  245.1 0.6 broadcast_multiply_fusion
  (26 shorter events, 0.9 us)
Async XLA Ops:
  7.2 29.7 %copy-start.1 = (bf16[16,2,128,128]{3,2,1,0:T(8,128)(2,1)S(1)}, bf16[16,2,128,128]{3,2,1,0:T(8,128)(2,1)}, u32[]{:S(2)}) copy-start(bf16[16,2,128,128]{3,2,1,0:T(8,128)(2,1)} %param.8) | copy-start | bytes 3145732
  36.8 1.5 copy-start.5
  38.4 2.7 %copy-start = (f32[16,128,192]{1,2,0:T(8,128)S(1)}, f32[16,128,192]{1,2,0:T(8,128)}, u32[]{:S(2)}) copy-start(f32[16,128,192]{1,2,0:T(8,128)} %convolution_bitcast_fusion) | copy-start | bytes 4718596
  45.6 25.0 %collective-permute-start.2 = (bf16[2048,192]{0,1:T(8,128)(2,1)S(1)}, bf16[2048,192]{0,1:T(8,128)(2,1)S(1)}, u32[]{:S(2)}, u32[]{:S(2)}) collective-permute-start(bf16[2048,192]{0,1:T(8,128)(2,1)S(1)} %bitcast.95), channel_id=1, source_target_pairs={{0,16},{16,32},{32,48},{48,64},{64,80},{80,96},{96,112},{112,128},... | collective-permute-start | bytes 2359304 | tf_op jit(solution)/shard_map/ppermute | solution.py:14
  49.0 22.8 %collective-permute-start.3 = (bf16[2048,192]{0,1:T(8,128)(2,1)S(1)}, bf16[2048,192]{0,1:T(8,128)(2,1)S(1)}, u32[]{:S(2)}, u32[]{:S(2)}) collective-permute-start(bf16[2048,192]{0,1:T(8,128)(2,1)S(1)} %bitcast.97), channel_id=1, source_target_pairs={{16,0},{32,16},{48,32},{64,48},{80,64},{96,80},{112,96},{128,112},... | collective-permute-start | bytes 2359304 | tf_op jit(solution)/shard_map/ppermute | solution.py:15
  74.3 4.7 %copy-start.3 = (bf16[128,192]{0,1:T(8,128)(2,1)S(1)}, bf16[128,192]{0,1:T(8,128)(2,1)}, u32[]{:S(2)}) copy-start(bf16[128,192]{0,1:T(8,128)(2,1)} %param.10) | copy-start | bytes 147460
  74.3 170.4 %all-to-all-start = ((bf16[3,16,128,192]{2,3,0,1:T(8,128)(2,1)}), bf16[3,16,128,192]{2,3,0,1:T(8,128)(2,1)S(1)}, u32[]{:S(2)}, u32[]{:S(2)}) async-start(bf16[3,16,128,192]{2,3,0,1:T(8,128)(2,1)} %copy.43), calls=%async_computation | async-start | bytes 4718592 | tf_op jit(solution)/shard_map/all_to_all | solution.py:68
  78.9 164.2 %reduce-scatter.4.cloned.1.call-start = ((), (), s32[]{:S(2)}) async-start(), calls=%async_computation.2 | async-start | bytes 1114112
  148.0 25.5 %collective-permute-start = (bf16[2048,192]{0,1:T(8,128)(2,1)}, bf16[2048,192]{0,1:T(8,128)(2,1)}, u32[]{:S(2)}, u32[]{:S(2)}) collective-permute-start(bf16[2048,192]{0,1:T(8,128)(2,1)} %all_gather.6), channel_id=1, source_target_pairs={{0,16},{16,32},{32,48},{48,64},{64,80},{80,96},{96,112},{112,128},... | collective-permute-start | bytes 2359304 | tf_op jit(solution)/shard_map/ppermute | solution.py:14
  149.9 24.5 %collective-permute-start.1 = (bf16[2048,192]{0,1:T(8,128)(2,1)}, bf16[2048,192]{0,1:T(8,128)(2,1)}, u32[]{:S(2)}, u32[]{:S(2)}) collective-permute-start(bf16[2048,192]{0,1:T(8,128)(2,1)} %all_gather.6), channel_id=1, source_target_pairs={{16,0},{32,16},{48,32},{64,48},{80,64},{96,80},{112,96},{128,112},... | collective-permute-start | bytes 2359304 | tf_op jit(solution)/shard_map/ppermute | solution.py:15
  190.6 53.4 %copy-start.2 = (f32[128,192]{0,1:T(8,128)S(1)}, f32[128,192]{0,1:T(8,128)}, u32[]{:S(2)}) copy-start(f32[128,192]{0,1:T(8,128)} %param.12) | copy-start | bytes 294916
  190.6 53.4 %copy-start.4 = (bf16[128,192]{0,1:T(8,128)(2,1)S(1)}, bf16[128,192]{0,1:T(8,128)(2,1)}, u32[]{:S(2)}) copy-start(bf16[128,192]{0,1:T(8,128)(2,1)} %param.11) | copy-start | bytes 147460
Sparse Core Ops, SparseCore 0:
  187.3 55.7 reduce-scatter.3
where the time goes:
time: 255 us; the launch traced here: 253 us
  blocking collectives  95.7 us (38%)
  waiting for transfers between devices  83.4 us (33%)
  starting transfers between devices  23.4 us (9%)
  matrix products  15.9 us (6%)
  between operations  15 us (6%)
  local copies, waits for them, and re-layouts  12.6 us (5%)
  other arithmetic  6.56 us (3%)
    all_gather x1, blocking collectives, per_device(): group_panel = lax.all_gather(panel_now, 'inner', axis=0, tiled=True)  69.1 us
    unnamed x2, waiting for transfers between devices  50.1 us
    ppermute x2, waiting for transfers between devices, with_halo(): before = lax.ppermute(last, axis, up)  31.3 us
    all_gather x1, blocking collectives, per_device(): cot_group = lax.all_gather(cot_total, 'inner', axis=0, tiled=True)  26.7 us
    ppermute x2, starting transfers between devices, with_halo(): after = lax.ppermute(first, axis, down)  13.6 us
    dot_general x2, matrix products, per_device(): jnp.einsum('rw,rjn->wjn', selector, back_slot, precision=lax.Precision.HI...  6.54 us
    unnamed x20, local copies, waits for them, and re-layouts  6.36 us
    ppermute x2, starting transfers between devices, with_halo(): before = lax.ppermute(last, axis, up)  5.12 us
  transfers between devices with their start and end apart: 6, of which 5 were waited for; matrix products, arithmetic and copies ran while one was open for 8% of the time, Pallas kernels for 0%

commit v1 on v0

v1 whole, which is shorter than its diff:
```python
import functools

import jax
import jax.numpy as jnp
from jax import lax
from jax.experimental import pallas as pl
from jax.experimental.pallas import tpu as pltpu
from jax.sharding import PartitionSpec as P

MESH = pl.DeviceIdType.MESH
F32 = jnp.float32
BF16 = jnp.bfloat16
NT = (((1,), (1,)), ((), ()))
NN = (((1,), (0,)), ((), ()))
TN = (((0,), (0,)), ((), ()))


def dot(a, b, dims):
    return lax.dot_general(a, b, dims, preferred_element_type=F32)


def kernel(
    rows, inner, meta, coeff, h, now, prev, dens, cotp, cotd,
    o_next, o_dens, o_grad, o_gh,
    hbuf, gbuf, v_now, v_prev, v_dens, v_cotp, v_cotd, v_next, v_dout, v_grad,
    win, cot, chain, tout, tsib, ysend, yrecv, pout, psib, rsend, rrecv,
    in_sem, out_sem, ring_s, ring_r, sib_s, sib_r, y_s, y_r, ysib_s, ysib_r,
    tsib_s, tsib_r, ty_s, ty_r, psib_s, psib_r, rs_s, rs_r,
):
    zs = inner // 2
    half = zs // 2
    nv, bs = win.shape[1:]
    lower, upper = pl.ds(0, nv // 2), pl.ds(nv // 2, nv // 2)
    part = (lower, upper)
    pairs = 2 * inner
    r = lax.axis_index("row")
    i = lax.axis_index("inner")
    z, c = i // 2, lax.rem(i, 2)
    o = 1 - c

    def at_z(step):
        return lax.rem(z + step + zs, zs)

    sibling = (r, 2 * z + o)
    along = ((r, 2 * at_z(1) + c), (r, 2 * at_z(-1) + c))
    row_up = (lax.rem(r + 1, rows), i)
    row_down = (lax.rem(r + rows - 1, rows), i)
    started = []

    def send(src, dst, s, v, device):
        copy = pltpu.make_async_remote_copy(
            src_ref=src, dst_ref=dst, send_sem=s, recv_sem=v,
            device_id=device, device_id_type=MESH,
        )
        copy.start()
        started.append(copy)
        return copy

    def pos(g, parity, zz):
        return (g * 2 + parity) * zs + zz

    loads = []
    for k, (src, dst) in enumerate(
        ((now, v_now), (cotp, v_cotp), (cotd, v_cotd), (h, hbuf), (prev, v_prev), (dens, v_dens))
    ):
        copy = pltpu.make_async_copy(src, dst, in_sem.at[k])
        copy.start()
        loads.append(copy)

    barrier = pltpu.get_barrier_semaphore()
    for device in (sibling, along[0], along[1], row_up, row_down):
        pl.semaphore_signal(barrier, inc=1, device_id=device, device_id_type=MESH)

    eye = (
        lax.broadcasted_iota(jnp.int32, (nv, nv), 0) == lax.broadcasted_iota(jnp.int32, (nv, nv), 1)
    ).astype(F32).astype(BF16)
    scale = coeff[0]
    loads[0].wait()
    win[pos(1, c, z)] = dot(eye, v_now[...], NT).astype(BF16)
    pl.semaphore_wait(barrier, 5)

    offs = [0]
    for k in range(1, half):
        offs += [-k, k]
    offs.append(half)

    held = (win, cot)
    base = (1, 0)
    ring = {}
    sib = {}
    ysent = {}

    def ring_send(a, way, step, off):
        ref = held[a].at[pos(base[a], c, at_z(off))]
        if step == half:
            ref = ref.at[part[way]]
        ring[a, way, step] = send(
            ref, ref, ring_s.at[a, way, step - 1], ring_r.at[a, way, step - 1], along[way]
        )

    def spread(a, j):
        zz = at_z(offs[j])
        src = held[a].at[pos(base[a], c, zz)]
        if a == 0:
            ysent[0, j] = send(src, win.at[pos(2, c, zz)], y_s.at[0, j], y_r.at[0, j], row_down)
            ysent[1, j] = send(src, win.at[pos(0, c, zz)], y_s.at[1, j], y_r.at[1, j], row_up)
        sib[a, j] = send(src, src, sib_s.at[a, j], sib_r.at[a, j], sibling)

    def own_out(a):
        ring_send(a, 0, 1, 0)
        ring_send(a, 1, 1, 0)
        spread(a, 0)

    own_out(0)
    loads[1].wait()
    loads[2].wait()
    total = (v_cotp[...].astype(F32) + scale * v_cotd[...].astype(F32)).astype(BF16)
    cot[pos(0, c, z)] = dot(eye, total, NT).astype(BF16)
    own_out(1)

    for k in range(1, half + 1):
        for a in range(2):
            for way in range(2):
                ring[a, way, k].wait_recv()
                if k < half:
                    ring_send(a, way, k + 1, -k if way == 0 else k)
                    spread(a, 2 * k - 1 + way)
            if k == half:
                spread(a, zs - 1)

    ysib = {}

    def y_forward(j):
        zz = at_z(offs[j])
        for way, g in ((0, 2), (1, 0)):
            ysent[way, j].wait_recv()
            ref = win.at[pos(g, c, zz)]
            ysib[way, j] = send(ref, ref, ysib_s.at[way, j], ysib_r.at[way, j], sibling)

    for j in range(half):
        y_forward(j)
    for j in range(zs):
        sib[1, j].wait_recv()
    loads[3].wait()

    chain[pairs] = jnp.zeros((nv, bs), F32)
    for b in range(inner):
        both = jnp.concatenate([hbuf[b, 0], hbuf[b, 1]], axis=1)
        back = dot(cot[pos(0, b % 2, b // 2)], both, NN)
        for s in range(2):
            p = 2 * b + s
            chain[p] = back[:, s * bs : (s + 1) * bs] + chain[meta[pairs + p]]

    def last(position):
        return chain[meta[2 * pairs + position]]

    tsent = {}
    for k, g in enumerate((0, 2, 1)):
        for zz in range(zs):
            tout[k, zz] = last(pos(g, o, zz)).astype(BF16)
        tsent[k] = send(tout.at[k], tsib.at[k], tsib_s.at[k], tsib_r.at[k], sibling)

    for j in range(half, zs):
        y_forward(j)

    far = [half]
    for k in range(half - 1, 0, -1):
        far += [k, -k]
    far.append(0)
    ty = {}
    tsent[0].wait_recv()
    tsent[1].wait_recv()
    for j, off in enumerate(far):
        zz = at_z(off)
        for k, g, device in ((0, 0, row_down), (1, 2, row_up)):
            ysend[k, zz] = (last(pos(g, c, zz)) + tsib[k, zz].astype(F32)).astype(BF16)
            ty[k, j] = send(
                ysend.at[k, zz], yrecv.at[k, zz], ty_s.at[k, j], ty_r.at[k, j], device
            )

    for j in range(zs):
        sib[0, j].wait_recv()
    for j in range(zs):
        for way in range(2):
            ysib[way, j].wait_recv()

    def picked(b):
        return jnp.concatenate([win[meta[2 * b]], win[meta[2 * b + 1]]], axis=1)

    def partial(b):
        both = jnp.concatenate([hbuf[b, 0], hbuf[b, 1]], axis=1)
        return dot(picked(b), both, NT)

    for b in range(inner):
        pout[pos(0, b % 2, b // 2)] = partial(b).astype(BF16)
    psent = send(
        pout.at[pl.ds(o * zs, zs)], psib, psib_s.at[0], psib_r.at[0], sibling
    )
    stores = []

    def grad_rows(first, count):
        for b in range(first, first + count):
            got = 2.0 * dot(cot[pos(0, b % 2, b // 2)], picked(b), TN)
            for s in range(2):
                gbuf[b, s] = got[:, s * bs : (s + 1) * bs].astype(BF16)
        span = pl.ds(first, count)
        copy = pltpu.make_async_copy(gbuf.at[span], o_gh.at[span], out_sem.at[len(stores)])
        copy.start()
        stores.append(copy)

    def term_here(off):
        j = far.index(off)
        for k in range(2):
            ty[k, j].wait_recv()
        zz = at_z(off)
        return (
            last(pos(1, c, zz)) + tsib[2, zz].astype(F32)
            + yrecv[0, zz].astype(F32) + yrecv[1, zz].astype(F32)
        )

    def product_here(off):
        zz = at_z(off)
        return pout[pos(0, c, zz)].astype(F32) + psib[zz].astype(F32)

    here = (product_here, term_here)
    rs = {}

    def rs_step(a, t):
        d = half + 1 - t
        shared = here[a](half) if t == 1 else None
        for way in range(2):
            out, got = rsend.at[a, way, t - 1], rrecv.at[a, way, t - 1]
            if t == 1:
                rows_here = part[way]
                start = way * (nv // 2)
                out[rows_here, :] = shared[start : start + nv // 2].astype(BF16)
                out, got = out.at[rows_here], got.at[rows_here]
            else:
                value = here[a](d if way == 0 else -d)
                rs[a, way, t - 1].wait_recv()
                if t == 2:
                    start = way * (nv // 2)
                    other = nv // 2 - start
                    out[part[way], :] = (
                        value[start : start + nv // 2]
                        + rrecv[a, way, 0, part[way], :].astype(F32)
                    ).astype(BF16)
                    out[part[1 - way], :] = value[other : other + nv // 2].astype(BF16)
                else:
                    out[...] = (value + rrecv[a, way, t - 2].astype(F32)).astype(BF16)
            rs[a, way, t] = send(
                out, got, rs_s.at[a, way, t - 1], rs_r.at[a, way, t - 1], along[way]
            )

    def finish(a):
        value = here[a](0)
        for way in range(2):
            rs[a, way, half].wait_recv()
            value = value + rrecv[a, way, half - 1].astype(F32)
        return value.T

    psent.wait_recv()
    tsent[2].wait_recv()
    chunk = inner // half
    for t in range(1, half + 1):
        rs_step(0, t)
        rs_step(1, t)
        grad_rows((t - 1) * chunk, chunk)

    loads[4].wait()
    loads[5].wait()
    nxt = (2.0 * finish(0) - v_prev[...].astype(F32)).astype(BF16)
    v_next[...] = nxt
    v_dout[...] = v_dens[...] + scale * nxt.astype(F32)
    for src, dst in ((v_next, o_next), (v_dout, o_dens)):
        copy = pltpu.make_async_copy(src, dst, out_sem.at[len(stores)])
        copy.start()
        stores.append(copy)
    v_grad[...] = 2.0 * finish(1)
    copy = pltpu.make_async_copy(v_grad, o_grad, out_sem.at[len(stores)])
    copy.start()
    stores.append(copy)
    for copy in stores:
        copy.wait()
    for copy in started:
        copy.wait_send()


def per_device(h, cols, now, prev, dens, coeff, cotp, cotd):
    inner, slots, bs, _ = h.shape
    nv = now.shape[1]
    rows = lax.axis_size("row")
    zs, half = inner // 2, inner // 4
    pairs = inner * slots
    first = lax.axis_index("row") * inner
    w = ((cols - first + inner) % (rows * inner)).reshape(pairs)
    g, ii = w // inner, w % inner
    where = (g * 2 + ii % 2) * zs + ii // 2
    q = jnp.arange(pairs, dtype=jnp.int32)
    targets = jnp.concatenate([where, jnp.arange(3 * inner, dtype=jnp.int32)])
    limit = jnp.concatenate([q, jnp.full((3 * inner,), pairs, jnp.int32)])
    hit = (targets[:, None] == where[None, :]) & (q[None, :] < limit[:, None])
    link = jnp.max(jnp.where(hit, q[None, :], -1), axis=1)
    link = jnp.where(link < 0, pairs, link)
    meta = jnp.concatenate([where, link])

    blk = (nv, bs)
    any_spec = pl.BlockSpec(memory_space=pl.ANY)
    smem = pl.BlockSpec(memory_space=pltpu.SMEM)
    vm = pltpu.VMEM
    sem = lambda *shape: pltpu.SemaphoreType.DMA(shape)
    scratch = [
        vm(h.shape, BF16), vm(h.shape, BF16),
        vm((bs, nv), BF16), vm((bs, nv), BF16), vm((bs, nv), F32), vm((bs, nv), BF16), vm((bs, nv), BF16),
        vm((bs, nv), BF16), vm((bs, nv), F32), vm((bs, nv), F32),
        vm((3 * inner, *blk), BF16), vm((inner, *blk), BF16), vm((pairs + 1, *blk), F32),
        vm((3, zs, *blk), BF16), vm((3, zs, *blk), BF16),
        vm((2, zs, *blk), BF16), vm((2, zs, *blk), BF16),
        vm((inner, *blk), BF16), vm((zs, *blk), BF16),
        vm((2, 2, half, *blk), BF16), vm((2, 2, half, *blk), BF16),
        sem(6), sem(half + 3), sem(2, 2, half), sem(2, 2, half), sem(2, zs), sem(2, zs),
        sem(2, zs), sem(2, zs), sem(2, zs), sem(2, zs),
        sem(3), sem(3), sem(2, zs), sem(2, zs), sem(1), sem(1), sem(2, 2, half), sem(2, 2, half),
    ]
    return pl.pallas_call(
        functools.partial(kernel, rows, inner),
        out_shape=(
            jax.ShapeDtypeStruct((bs, nv), BF16),
            jax.ShapeDtypeStruct((bs, nv), F32),
            jax.ShapeDtypeStruct((bs, nv), F32),
            jax.ShapeDtypeStruct(h.shape, BF16),
        ),
        in_specs=[smem, smem] + [any_spec] * 6,
        out_specs=(any_spec,) * 4,
        scratch_shapes=scratch,
        compiler_params=pltpu.CompilerParams(
            collective_id=0, has_side_effects=True, vmem_limit_bytes=40 * 1024 * 1024
        ),
        cost_estimate=pl.CostEstimate(
            flops=6 * pairs * bs * bs * nv, bytes_accessed=4 * h.size + 20 * bs * nv, transcendentals=0
        ),
    )(meta, coeff, h, now, prev, dens, cotp, cotd)


def solution(mesh):
    both = P(("row", "inner"), None)
    blocks = P("row", "inner", None, None)
    return jax.shard_map(
        per_device,
        mesh=mesh,
        in_specs=(blocks, P("row", "inner"), both, both, both, P(), both, both),
        out_specs=(both, both, both, blocks),
        check_vma=False,
    )
```

time: 255 us -> 62.3 us (0.24)
  the two profiles are of different devices: /device:TPU:1 before, /device:TPU:64 now
where the time goes in v1:
time: 62.3 us; the launch traced here: 61.9 us
  Pallas kernels  52.4 us (84%)
  local copies, waits for them, and re-layouts  7.8 us (13%)
  between operations  1.42 us (2%)
    pallas_call x1, Pallas kernels, per_device(): pl.pallas_call(functools.partial(kernel, rows, inner), out_shape=(jax.Sha...  52.4 us
    unnamed x20, local copies, waits for them, and re-layouts  5.43 us
    pallas_call x3, local copies, waits for them, and re-layouts, per_device(): pl.pallas_call(functools.partial(kernel, rows, inner), out_shape=(jax.Sha...  2.2 us

profile of v1, /device:TPU:64, one launch (start us, length us, event | category | flops | bytes accessed | tf_op | source)
XLA Modules:
  0.0 61.9 jit_solution(6478333143550956434)
XLA Ops:
  0.6 0.0 copy-start.5
  1.3 0.0 copy-done.5
  1.3 0.1 copy.30
  1.4 0.1 reshape.91
  1.5 0.0 copy-start.6
  1.6 0.1 pad_add_fusion
  1.6 0.6 copy-done.6
  2.2 0.1 select_reduce_fusion
  2.3 0.1 pad_add_fusion.1.meta
  2.4 0.0 copy-start.2
  2.4 0.9 %copy.31.now = bf16[128,192]{1,0:T(8,128)(2,1)S(1)} copy(bf16[128,192]{0,1:T(8,128)(2,1)} %param.10) | data formatting | bytes 98304 | tf_op args[2]
  3.3 0.0 copy-done.2
  3.3 0.0 copy-start.3
  3.3 0.0 copy-start.4
  3.3 0.1 copy.32.prev
  3.4 0.7 %copy-done.3 = bf16[128,192]{0,1:T(8,128)(2,1)S(1)} copy-done((bf16[128,192]{0,1:T(8,128)(2,1)S(1)}, bf16[128,192]{0,1:T(8,128)(2,1)}, u32[]{:S(2)}) %copy-start.3) | copy-done | bytes 49176
  4.1 0.0 copy-start.1
  4.1 0.1 copy.34.cotp
  4.2 0.0 copy-done.4
  4.2 0.1 copy.35.cotd
  4.3 0.7 %copy-done.1 = f32[128,192]{0,1:T(8,128)S(1)} copy-done((f32[128,192]{0,1:T(8,128)S(1)}, f32[128,192]{0,1:T(8,128)}, u32[]{:S(2)}) %copy-start.1) | copy-done | bytes 98328
  5.0 0.1 copy.33.dens
  5.1 0.0 copy-start
  5.1 1.2 %copy-done = bf16[16,2,128,128]{3,2,1,0:T(8,128)(2,1)S(1)} copy-done((bf16[16,2,128,128]{3,2,1,0:T(8,128)(2,1)S(1)}, bf16[16,2,128,128]{3,2,1,0:T(8,128)(2,1)}, u32[]{:S(2)}) %copy-start) | copy-done | bytes 1048600
  6.3 52.4 %shard_map.111 = (bf16[128,192]{1,0:T(8,128)(2,1)S(1)}, f32[128,192]{1,0:T(8,128)S(1)}, f32[128,192]{1,0:T(8,128)S(1)}, bf16[16,2,128,128]{3,2,1,0:T(8,128)(2,1)S(1)}) custom-call(s32[112]{0:T(128)S(1)} %pad_add_fusion.1.meta, f32[1]{0:T(128)S(6)} %copy.40.coeff, bf16[16,2,128,128]{3,2,1,0:T(8,128)(2,1)S(1)} %copy-done, bf16[128,192]{1,0:T(8,128)(2,1)S(1)} %copy.31.now, ...), custom_call_target="tpu_custom_call" | custom-call | flops 603979776 | bytes 2588672 | tf_op jit(solution)/shard_map/pallas_call | solution.py:325
  58.8 0.7 %copy.36 = bf16[128,192]{0,1:T(8,128)(2,1)} copy(bf16[128,192]{1,0:T(8,128)(2,1)S(1)} %get-tuple-element.12) | data formatting | bytes 98304 | tf_op jit(solution)/shard_map/pallas_call | solution.py:325
  59.5 0.7 %copy.37 = f32[128,192]{0,1:T(8,128)} copy(f32[128,192]{1,0:T(8,128)S(1)} %get-tuple-element.13) | data formatting | bytes 196608 | tf_op jit(solution)/shard_map/pallas_call | solution.py:325
  60.2 0.7 %copy.38 = f32[128,192]{0,1:T(8,128)} copy(f32[128,192]{1,0:T(8,128)S(1)} %get-tuple-element.14) | data formatting | bytes 196608 | tf_op jit(solution)/shard_map/pallas_call | solution.py:325
  61.0 1.0 %copy.41 = bf16[16,2,128,128]{3,2,1,0:T(8,128)(2,1)} copy(bf16[16,2,128,128]{3,2,1,0:T(8,128)(2,1)S(1)} %get-tuple-element.23) | data formatting | bytes 2097152
  (4 shorter events, 0.0 us)
Async XLA Ops:
  0.6 0.7 %copy-start.5 = (s32[16,2]{0,1:T(2,128)S(1)}, s32[16,2]{0,1:T(2,128)}, u32[]{:S(2)}) copy-start(s32[16,2]{0,1:T(2,128)} %param.9) | copy-start | bytes 388
  1.5 0.7 %copy-start.6 = (s32[80]{0:T(128)S(1)}, s32[80]{0:T(128)}, u32[]{:S(2)}) copy-start(s32[80]{0:T(128)} %constant.80.clone.1) | copy-start | bytes 964
  2.4 0.9 %copy-start.2 = (bf16[128,192]{0,1:T(8,128)(2,1)S(1)}, bf16[128,192]{0,1:T(8,128)(2,1)}, u32[]{:S(2)}) copy-start(bf16[128,192]{0,1:T(8,128)(2,1)} %param.11) | copy-start | bytes 147460
  3.3 0.8 %copy-start.3 = (bf16[128,192]{0,1:T(8,128)(2,1)S(1)}, bf16[128,192]{0,1:T(8,128)(2,1)}, u32[]{:S(2)}) copy-start(bf16[128,192]{0,1:T(8,128)(2,1)} %param.14) | copy-start | bytes 147460
  3.3 0.9 %copy-start.4 = (bf16[128,192]{0,1:T(8,128)(2,1)S(1)}, bf16[128,192]{0,1:T(8,128)(2,1)}, u32[]{:S(2)}) copy-start(bf16[128,192]{0,1:T(8,128)(2,1)} %param.15) | copy-start | bytes 147460
  4.1 0.9 %copy-start.1 = (f32[128,192]{0,1:T(8,128)S(1)}, f32[128,192]{0,1:T(8,128)}, u32[]{:S(2)}) copy-start(f32[128,192]{0,1:T(8,128)} %param.12) | copy-start | bytes 294916
  5.1 1.2 %copy-start = (bf16[16,2,128,128]{3,2,1,0:T(8,128)(2,1)S(1)}, bf16[16,2,128,128]{3,2,1,0:T(8,128)(2,1)}, u32[]{:S(2)}) copy-start(bf16[16,2,128,128]{3,2,1,0:T(8,128)(2,1)} %h.1) | copy-start | bytes 3145732

commit v2 on v1

--- a/solution.py
+++ b/solution.py
@@ -71,12 +71,9 @@
     for device in (sibling, along[0], along[1], row_up, row_down):
         pl.semaphore_signal(barrier, inc=1, device_id=device, device_id_type=MESH)
 
-    eye = (
-        lax.broadcasted_iota(jnp.int32, (nv, nv), 0) == lax.broadcasted_iota(jnp.int32, (nv, nv), 1)
-    ).astype(F32).astype(BF16)
     scale = coeff[0]
     loads[0].wait()
-    win[pos(1, c, z)] = dot(eye, v_now[...], NT).astype(BF16)
+    win[pos(1, c, z)] = v_now[...]
     pl.semaphore_wait(barrier, 5)
 
     offs = [0]
@@ -115,7 +112,7 @@
     loads[1].wait()
     loads[2].wait()
     total = (v_cotp[...].astype(F32) + scale * v_cotd[...].astype(F32)).astype(BF16)
-    cot[pos(0, c, z)] = dot(eye, total, NT).astype(BF16)
+    cot[pos(0, c, z)] = total
     own_out(1)
 
     for k in range(1, half + 1):
@@ -257,7 +254,7 @@
         for way in range(2):
             rs[a, way, half].wait_recv()
             value = value + rrecv[a, way, half - 1].astype(F32)
-        return value.T
+        return value
 
     psent.wait_recv()
     tsent[2].wait_recv()
@@ -311,8 +308,8 @@
     sem = lambda *shape: pltpu.SemaphoreType.DMA(shape)
     scratch = [
         vm(h.shape, BF16), vm(h.shape, BF16),
-        vm((bs, nv), BF16), vm((bs, nv), BF16), vm((bs, nv), F32), vm((bs, nv), BF16), vm((bs, nv), BF16),
-        vm((bs, nv), BF16), vm((bs, nv), F32), vm((bs, nv), F32),
+        vm(blk, BF16), vm(blk, BF16), vm(blk, F32), vm(blk, BF16), vm(blk, BF16),
+        vm(blk, BF16), vm(blk, F32), vm(blk, F32),
         vm((3 * inner, *blk), BF16), vm((inner, *blk), BF16), vm((pairs + 1, *blk), F32),
         vm((3, zs, *blk), BF16), vm((3, zs, *blk), BF16),
         vm((2, zs, *blk), BF16), vm((2, zs, *blk), BF16),
@@ -322,24 +319,25 @@
         sem(2, zs), sem(2, zs), sem(2, zs), sem(2, zs),
         sem(3), sem(3), sem(2, zs), sem(2, zs), sem(1), sem(1), sem(2, 2, half), sem(2, 2, half),
     ]
-    return pl.pallas_call(
+    out = pl.pallas_call(
         functools.partial(kernel, rows, inner),
         out_shape=(
-            jax.ShapeDtypeStruct((bs, nv), BF16),
-            jax.ShapeDtypeStruct((bs, nv), F32),
-            jax.ShapeDtypeStruct((bs, nv), F32),
+            jax.ShapeDtypeStruct(blk, BF16),
+            jax.ShapeDtypeStruct(blk, F32),
+            jax.ShapeDtypeStruct(blk, F32),
             jax.ShapeDtypeStruct(h.shape, BF16),
         ),
         in_specs=[smem, smem] + [any_spec] * 6,
         out_specs=(any_spec,) * 4,
         scratch_shapes=scratch,
         compiler_params=pltpu.CompilerParams(
-            collective_id=0, has_side_effects=True, vmem_limit_bytes=40 * 1024 * 1024
+            collective_id=0, has_side_effects=True, vmem_limit_bytes=60 * 1024 * 1024
         ),
         cost_estimate=pl.CostEstimate(
             flops=6 * pairs * bs * bs * nv, bytes_accessed=4 * h.size + 20 * bs * nv, transcendentals=0
         ),
-    )(meta, coeff, h, now, prev, dens, cotp, cotd)
+    )(meta, coeff, h, now.T, prev.T, dens.T, cotp.T, cotd.T)
+    return (out[0].T, out[1].T, out[2].T, out[3])
 
 
 def solution(mesh):

time: 62.3 us -> 61.5 us (0.987)
  local copies, waits for them, and re-layouts: 7.8 us -> 6.75 us
    pallas_call x3 -> x0, local copies, waits for them, and re-layouts: 2.2 us -> none  [per_device(): pl.pallas_call(functools.partial(kernel, rows, inner), out_shape=(jax.Sha...]
    unnamed x20 -> x12, local copies, waits for them, and re-layouts: 5.43 us -> 6.58 us
where the time goes in v2:
time: 61.5 us; the launch traced here: 61.2 us
  Pallas kernels  52.3 us (85%)
  local copies, waits for them, and re-layouts  6.75 us (11%)
  between operations  1.33 us (2%)
  other arithmetic  0.79 us (1%)
    pallas_call x1, Pallas kernels, per_device(): pl.pallas_call(functools.partial(kernel, rows, inner), out_shape=(jax.Sha...  52.3 us
    unnamed x12, local copies, waits for them, and re-layouts  6.58 us

profile of v2, /device:TPU:64, one launch (start us, length us, event | category | flops | bytes accessed | tf_op | source)
XLA Modules:
  0.0 61.2 jit_solution(4652196158619137859)
XLA Ops:
  1.3 0.0 copy-start.2
  1.3 0.7 %copy-done.2 = s32[16,2]{0,1:T(2,128)S(1)} copy-done((s32[16,2]{0,1:T(2,128)S(1)}, s32[16,2]{0,1:T(2,128)}, u32[]{:S(2)}) %copy-start.2) | copy-done | bytes 152
  2.0 0.1 copy.14
  2.1 0.1 reshape.91
  2.2 0.0 copy-start.3
  2.2 0.1 pad_add_fusion
  2.3 0.6 copy-done.3
  2.8 0.1 select_reduce_fusion
  2.9 0.6 pad_add_fusion.1.meta
  3.5 52.3 %shard_map.111 = (bf16[192,128]{1,0:T(8,128)(2,1)}, f32[192,128]{1,0:T(8,128)}, f32[192,128]{1,0:T(8,128)}, bf16[16,2,128,128]{3,2,1,0:T(8,128)(2,1)}) custom-call(s32[112]{0:T(128)} %pad_add_fusion.1.meta, f32[1]{0:T(128)S(6)} %copy.19.coeff, bf16[16,2,128,128]{3,2,1,0:T(8,128)(2,1)} %h.1, bf16[192,128]{1,0:T(8,128)(2,1)} %bitcast.12, ...), custom_call_target="tpu_custom_call" | custom-call | flops 603979776 | bytes 2588672 | tf_op jit(solution)/shard_map/pallas_call | solution.py:322
  55.8 0.0 copy-start.1
  55.9 1.5 %copy.20 = bf16[128,192]{0,1:T(8,128)(2,1)} copy(bf16[128,192]{0,1:T(8,128)(2,1)} %bitcast.10) | data formatting | bytes 98304
  57.3 0.0 copy-done.1
  57.3 0.0 copy-start
  57.3 0.6 %copy.21 = f32[128,192]{0,1:T(8,128)} copy(f32[128,192]{0,1:T(8,128)S(1)} %bitcast.9) | data formatting | bytes 196608
  58.0 0.3 copy-done
  58.2 0.6 %copy.22 = f32[128,192]{0,1:T(8,128)} copy(f32[128,192]{0,1:T(8,128)S(1)} %bitcast.8) | data formatting | bytes 196608
  58.9 2.3 %copy.23 = bf16[16,2,128,128]{3,2,1,0:T(8,128)(2,1)} copy(bf16[16,2,128,128]{3,2,1,0:T(8,128)(2,1)} %get-tuple-element.19) | data formatting | bytes 2097152
  (4 shorter events, 0.0 us)
Async XLA Ops:
  1.3 0.7 %copy-start.2 = (s32[16,2]{0,1:T(2,128)S(1)}, s32[16,2]{0,1:T(2,128)}, u32[]{:S(2)}) copy-start(s32[16,2]{0,1:T(2,128)} %param.9) | copy-start | bytes 388
  2.2 0.7 %copy-start.3 = (s32[80]{0:T(128)S(1)}, s32[80]{0:T(128)}, u32[]{:S(2)}) copy-start(s32[80]{0:T(128)} %constant.80.clone.1) | copy-start | bytes 964
  55.8 1.5 %copy-start.1 = (f32[192,128]{1,0:T(8,128)S(1)}, f32[192,128]{1,0:T(8,128)}, u32[]{:S(2)}) copy-start(f32[192,128]{1,0:T(8,128)} %get-tuple-element.9) | copy-start | bytes 294916
  57.3 0.9 %copy-start = (f32[192,128]{1,0:T(8,128)S(1)}, f32[192,128]{1,0:T(8,128)}, u32[]{:S(2)}) copy-start(f32[192,128]{1,0:T(8,128)} %get-tuple-element.10) | copy-start | bytes 294916

commit v3 on v2

v3 whole, which is shorter than its diff:
```python
import functools

import jax
import jax.numpy as jnp
from jax import lax
from jax.experimental import pallas as pl
from jax.experimental.pallas import tpu as pltpu
from jax.sharding import PartitionSpec as P

MESH = pl.DeviceIdType.MESH
F32 = jnp.float32
BF16 = jnp.bfloat16
NT = (((1,), (1,)), ((), ()))
NN = (((1,), (0,)), ((), ()))
TN = (((0,), (0,)), ((), ()))


def dot(a, b, dims):
    return lax.dot_general(a, b, dims, preferred_element_type=F32)


def kernel(
    rows, inner, cols, coeff, h, now, prev, dens, cotp, cotd,
    o_next, o_dens, o_grad, o_gh,
    hbuf, gbuf, v_prev, v_dens, v_cotp, v_cotd, v_next, v_dout, v_grad,
    win, cot, chain, tout, tsib, ysend, yrecv, pout, psib, rsend, rrecv,
    where, link, last,
    in_sem, out_sem, ring_s, ring_r, sib_s, sib_r, y_s, y_r, ysib_s, ysib_r,
    tsib_s, tsib_r, ty_s, ty_r, psib_s, psib_r, rs_s, rs_r,
):
    zs = inner // 2
    half = zs // 2
    nv, bs = win.shape[1:]
    part = (pl.ds(0, nv // 2), pl.ds(nv // 2, nv // 2))
    pairs = 2 * inner
    total_blocks = rows * inner
    r = lax.axis_index("row")
    i = lax.axis_index("inner")
    z, c = i // 2, lax.rem(i, 2)
    o = 1 - c

    offs = [0]
    for k in range(1, half):
        offs += [-k, k]
    offs.append(half)

    def at_z(step):
        return lax.rem(z + step + zs, zs)

    sibling = (r, 2 * z + o)
    along = ((r, 2 * at_z(1) + c), (r, 2 * at_z(-1) + c))
    row_up = (lax.rem(r + 1, rows), i)
    row_down = (lax.rem(r + rows - 1, rows), i)
    started = []

    def send(src, dst, s, v, device):
        copy = pltpu.make_async_remote_copy(
            src_ref=src, dst_ref=dst, send_sem=s, recv_sem=v,
            device_id=device, device_id_type=MESH,
        )
        copy.start()
        started.append(copy)
        return copy

    def pos(g, parity, j=0):
        return (g * 2 + parity) * zs + j

    def run(g, parity, span):
        return pl.ds(pos(g, parity, span[0]), span[1])

    loads = []
    for k, (src, dst) in enumerate(
        ((now, win.at[pos(1, c)]), (cotp, v_cotp), (cotd, v_cotd), (h, hbuf), (prev, v_prev), (dens, v_dens))
    ):
        copy = pltpu.make_async_copy(src, dst, in_sem.at[k])
        copy.start()
        loads.append(copy)

    barrier = pltpu.get_barrier_semaphore()
    for device in (sibling, along[0], along[1], row_up, row_down):
        pl.semaphore_signal(barrier, inc=1, device_id=device, device_id_type=MESH)

    scale = coeff[0]
    loads[1].wait()
    loads[2].wait()
    cot[pos(0, c)] = (v_cotp[...].astype(F32) + scale * v_cotd[...].astype(F32)).astype(BF16)
    loads[0].wait()
    pl.semaphore_wait(barrier, 5)

    held = (win, cot)
    base = (1, 0)
    ring = {}
    sib = {}
    ysent = {}
    spans = [(0, 1)] + [(2 * k - 1, 2) for k in range(1, half)] + [(zs - 1, 1)]

    def ring_send(a, way, step, p):
        j = 0 if step == 1 else 2 * (step - 1) - 1 + way
        came = 0 if step == 1 else (zs - 1 if step > half else j)
        goes = zs - 1 if step == half else 2 * step - 1 + way
        src = held[a].at[pos(base[a], c, came)].at[part[p]]
        dst = held[a].at[pos(base[a], c, goes)].at[part[p]]
        ring[a, way, step, p] = send(
            src, dst, ring_s.at[a, way, step - 1, p], ring_r.at[a, way, step - 1, p], along[way]
        )

    def ring_out(a, step):
        for p in range(2):
            for way in range(2):
                if step < half or p == way:
                    ring_send(a, way, step, p)

    def ring_on(a, k):
        for p in range(2):
            for way in range(2):
                if k == half and p != way:
                    continue
                ring[a, way, k, p].wait_recv()
                if k < half - 1 or (k == half - 1 and p == way):
                    ring_send(a, way, k + 1, p)

    def to_sibling(a, n):
        ref = held[a].at[run(base[a], c, spans[n])]
        sib[a, n] = send(ref, ref, sib_s.at[a, n], sib_r.at[a, n], sibling)

    def to_rows(n):
        src = win.at[run(1, c, spans[n])]
        for way, g, device in ((0, 2, row_down), (1, 0, row_up)):
            ysent[way, n] = send(
                src, win.at[run(g, c, spans[n])], y_s.at[way, n], y_r.at[way, n], device
            )

    ring_out(1, 1)
    to_rows(0)
    to_sibling(1, 0)
    ring_out(0, 1)

    def block_of(j, parity):
        return 2 * at_z(offs[j]) + parity

    uses = []
    for begin, count in spans:
        for whose in range(2):
            uses += [(j, whose) for j in range(begin, begin + count)]
    parities = (c, o)

    first = r * inner
    for n, (j, whose) in enumerate(uses):
        b = block_of(j, parities[whose])
        for s in range(2):
            w = lax.rem(cols[s, b] - first + inner + total_blocks, total_blocks)
            w = jnp.minimum(w, 3 * inner - 1)
            g, ii = w // inner, lax.rem(w, inner)
            rel = lax.rem(ii // 2 - z + zs, zs)
            jj = jnp.where(rel <= half, jnp.minimum(2 * rel, zs - 1), 2 * (zs - rel) - 1)
            where[2 * n + s] = pos(g, lax.rem(ii, 2), jj)

    def find(value, stop):
        found = jnp.int32(pairs)
        for q in range(stop):
            found = jnp.where(where[q] == value, q, found)
        return found

    def find_links(n):
        for q in (2 * n, 2 * n + 1):
            link[q] = find(where[q], 2 * n)

    def find_last(begin, end):
        def body(k, carry):
            last[k] = find(k, pairs)
            return carry

        lax.fori_loop(begin, end, body, 0)

    chain[pairs] = jnp.zeros((nv, bs), F32)

    def hcat(b):
        return jnp.concatenate([hbuf[b, 0], hbuf[b, 1]], axis=1)

    def back(n, j, parity):
        find_links(n)
        got = dot(cot[pos(0, parity, j)], hcat(block_of(j, parity)), NN)
        for s in range(2):
            q = 2 * n + s
            chain[q] = got[:, s * bs : (s + 1) * bs] + chain[link[q]]

    def backs(n, whose):
        begin, count = spans[n]
        for j in range(begin, begin + count):
            back(uses.index((j, whose)), j, parities[whose])

    ysib = {}
    packs = ((0, half + 1), (half + 1, half - 1))

    def y_wait(n):
        for way in range(2):
            ysent[way, n].wait_recv()

    def pack_out(m):
        for way, g in ((0, 2), (1, 0)):
            ref = win.at[run(g, c, packs[m])]
            ysib[way, m] = send(ref, ref, ysib_s.at[way, m], ysib_r.at[way, m], sibling)
        ref = win.at[run(1, c, packs[m])]
        ysib[2, m] = send(ref, ref, ysib_s.at[2, m], ysib_r.at[2, m], sibling)

    share = 3 * inner // half
    loads[3].wait()
    for k in range(1, half + 1):
        ring_on(1, k)
        to_sibling(1, k)
        if k == 1:
            backs(0, 0)
        ring_on(0, k)
        to_rows(k)
        if k < half:
            find_last((k - 1) * share, k * share)
        sib[1, k - 1].wait_recv()
        backs(k - 1, 1)
        backs(k, 0)
    find_last((half - 1) * share, half * share)
    sib[1, half].wait_recv()
    backs(half, 1)

    def tail(g, parity, j):
        return chain[last[pos(g, parity, j)]]

    cuts = ((zs - 3, 3), (zs - 5, 2), (0, zs - 5))
    tsent = {}

    def tails_out(k, g, m):
        begin, count = cuts[m]
        for j in range(begin, begin + count):
            tout[k, j] = tail(g, o, j).astype(BF16)
        span = pl.ds(begin, count)
        tsent[k, m] = send(
            tout.at[k, span], tsib.at[k, span], tsib_s.at[k, m], tsib_r.at[k, m], sibling
        )

    for m in range(3):
        tails_out(0, 0, m)
        tails_out(1, 2, m)

    for n in range(half):
        y_wait(n)
        if n == half // 2:
            pack_out(0)

    ty = {}

    def to_owners(n):
        begin, count = spans[n]
        for k, g, device in ((0, 0, row_down), (1, 2, row_up)):
            for j in range(begin, begin + count):
                ysend[k, j] = (tail(g, c, j) + tsib[k, j].astype(F32)).astype(BF16)
            span = pl.ds(begin, count)
            ty[k, n] = send(
                ysend.at[k, span], yrecv.at[k, span], ty_s.at[k, n], ty_r.at[k, n], device
            )

    ready = {half: 0, half - 2: 1, half - 3: 2}
    for n in range(half, -1, -1):
        if n in ready:
            tsent[0, ready[n]].wait_recv()
            tsent[1, ready[n]].wait_recv()
        to_owners(n)
        if n == half - 1:
            y_wait(half)
            pack_out(1)
    for m in range(3):
        tails_out(2, 1, m)
    for m in range(2):
        for way in range(3):
            ysib[way, m].wait_recv()

    def picked(n):
        return jnp.concatenate([win[where[2 * n]], win[where[2 * n + 1]]], axis=1)

    def product(n, j, parity, k):
        pout[k, j] = dot(picked(n), hcat(block_of(j, parity)), NT).astype(BF16)

    psent = {}
    for m in range(3):
        begin, count = cuts[m]
        for j in range(begin, begin + count):
            product(uses.index((j, 1)), j, o, 1)
        span = pl.ds(begin, count)
        psent[m] = send(pout.at[1, span], psib.at[span], psib_s.at[m], psib_r.at[m], sibling)
    for j in range(zs - 1, -1, -1):
        product(uses.index((j, 0)), j, c, 0)

    stores = []

    def store(src, dst):
        copy = pltpu.make_async_copy(src, dst, out_sem.at[len(stores)])
        copy.start()
        stores.append(copy)

    def grad_rows(begin, count):
        for n in range(begin, begin + count):
            j, parity = uses[n][0], parities[uses[n][1]]
            b = block_of(j, parity)
            got = 2.0 * dot(cot[pos(0, parity, j)], picked(n), TN)
            for s in range(2):
                gbuf[b, s] = got[:, s * bs : (s + 1) * bs].astype(BF16)

    def half_of(ref, p):
        return ref[part[p], :].astype(F32)

    def product_here(j, p):
        return half_of(pout.at[0, j], p) + half_of(psib.at[j], p)

    def term_here(j, p):
        spot = chain.at[last[pos(1, c, j)]]
        return (
            spot[part[p], :] + half_of(tsib.at[2, j], p)
            + half_of(yrecv.at[0, j], p) + half_of(yrecv.at[1, j], p)
        )

    here = (product_here, term_here)
    rs = {}

    def rs_step(a, t):
        d = half + 1 - t
        if a == 1:
            for k in range(2):
                ty[k, d].wait_recv()
        for turn in range(2):
            for way in range(2):
                p = way if turn else 1 - way
                if t == 1 and p != way:
                    continue
                j = zs - 1 if t == 1 else 2 * d - 1 + (1 - way)
                value = here[a](j, p)
                if t > 2 or (t == 2 and p == way):
                    rs[a, way, t - 1, p].wait_recv()
                    value = value + half_of(rrecv.at[a, way, t - 2], p)
                out = rsend.at[a, way, t - 1]
                out[part[p], :] = value.astype(BF16)
                rs[a, way, t, p] = send(
                    out.at[part[p]], rrecv.at[a, way, t - 1].at[part[p]],
                    rs_s.at[a, way, t - 1, p], rs_r.at[a, way, t - 1, p], along[way],
                )

    def finish(a, p):
        value = here[a](0, p)
        for way in range(2):
            rs[a, way, half, p].wait_recv()
            value = value + half_of(rrecv.at[a, way, half - 1], p)
        return value

    pneed = {1: 0, 3: 1, 4: 2}
    chunk = inner // half
    for t in range(1, half + 1):
        if t in pneed:
            psent[pneed[t]].wait_recv()
            tsent[2, pneed[t]].wait_recv()
        rs_step(0, t)
        rs_step(1, t)
        grad_rows((t - 1) * chunk, chunk)
    store(gbuf, o_gh)

    loads[4].wait()
    loads[5].wait()
    for p in range(2):
        nxt = (2.0 * finish(0, p) - half_of(v_prev, p)).astype(BF16)
        v_next[part[p], :] = nxt
        v_dout[part[p], :] = v_dens[part[p], :] + scale * nxt.astype(F32)
    store(v_next, o_next)
    store(v_dout, o_dens)
    for k in range(2):
        ty[k, 0].wait_recv()
    for p in range(2):
        v_grad[part[p], :] = 2.0 * finish(1, p)
    store(v_grad, o_grad)
    for copy in stores:
        copy.wait()
    for copy in started:
        copy.wait_send()


def per_device(h, cols, now, prev, dens, coeff, cotp, cotd):
    inner, slots, bs, _ = h.shape
    nv = now.shape[1]
    rows = lax.axis_size("row")
    zs, half = inner // 2, inner // 4
    pairs = inner * slots
    blk = (nv, bs)
    any_spec = pl.BlockSpec(memory_space=pl.ANY)
    hbm = pl.BlockSpec(memory_space=pltpu.HBM)
    smem = pl.BlockSpec(memory_space=pltpu.SMEM)
    vm = pltpu.VMEM
    sem = lambda *shape: pltpu.SemaphoreType.DMA(shape)
    scratch = [
        vm(h.shape, BF16), vm(h.shape, BF16),
        vm(blk, BF16), vm(blk, F32), vm(blk, BF16), vm(blk, BF16),
        vm(blk, BF16), vm(blk, F32), vm(blk, F32),
        vm((3 * inner, *blk), BF16), vm((inner, *blk), BF16), vm((pairs + 1, *blk), F32),
        vm((3, zs, *blk), BF16), vm((3, zs, *blk), BF16),
        vm((2, zs, *blk), BF16), vm((2, zs, *blk), BF16),
        vm((2, zs, *blk), BF16), vm((zs, *blk), BF16),
        vm((2, 2, half, *blk), BF16), vm((2, 2, half, *blk), BF16),
        pltpu.SMEM((pairs,), jnp.int32), pltpu.SMEM((pairs,), jnp.int32),
        pltpu.SMEM((3 * inner,), jnp.int32),
        sem(6), sem(4), sem(2, 2, half, 2), sem(2, 2, half, 2), sem(2, half + 1), sem(2, half + 1),
        sem(2, half + 1), sem(2, half + 1), sem(3, 2), sem(3, 2),
        sem(3, 3), sem(3, 3), sem(2, half + 1), sem(2, half + 1), sem(3), sem(3),
        sem(2, 2, half, 2), sem(2, 2, half, 2),
    ]
    out = pl.pallas_call(
        functools.partial(kernel, rows, inner),
        out_shape=(
            jax.ShapeDtypeStruct(blk, BF16),
            jax.ShapeDtypeStruct(blk, F32),
            jax.ShapeDtypeStruct(blk, F32),
            jax.ShapeDtypeStruct(h.shape, BF16),
        ),
        in_specs=[smem, smem] + [hbm] * 6,
        out_specs=(any_spec,) * 4,
        scratch_shapes=scratch,
        compiler_params=pltpu.CompilerParams(
            collective_id=0, has_side_effects=True, vmem_limit_bytes=40 * 1024 * 1024
        ),
        cost_estimate=pl.CostEstimate(
            flops=6 * pairs * bs * bs * nv, bytes_accessed=4 * h.size + 20 * bs * nv, transcendentals=0
        ),
    )(pltpu.with_memory_space_constraint(cols.T, pltpu.HBM), coeff, *[pltpu.with_memory_space_constraint(x, pltpu.HBM) for x in (h, now.T, prev.T, dens.T, cotp.T, cotd.T)])
    return (out[0].T, out[1].T, out[2].T, out[3])


def solution(mesh):
    both = P(("row", "inner"), None)
    blocks = P("row", "inner", None, None)
    return jax.shard_map(
        per_device,
        mesh=mesh,
        in_specs=(blocks, P("row", "inner"), both, both, both, P(), both, both),
        out_specs=(both, both, both, blocks),
        check_vma=False,
    )
```

time: 61.5 us -> 54.8 us (0.89)
  the two profiles are of different devices: /device:TPU:64 before, /device:TPU:1 now
where the time goes in v3:
time: 54.8 us; the launch traced here: 54.7 us
  Pallas kernels  50.5 us (92%)
  local copies, waits for them, and re-layouts  2.87 us (5%)
  between operations  1.29 us (2%)
    pallas_call x1, Pallas kernels, per_device(): pl.pallas_call(functools.partial(kernel, rows, inner), out_shape=(jax.Sha...  50.5 us
    unnamed x4, local copies, waits for them, and re-layouts  2.87 us

profile of v3, /device:TPU:1, one launch (start us, length us, event | category | flops | bytes accessed | tf_op | source)
XLA Modules:
  0.0 54.7 jit_solution(5924849018640512905)
XLA Ops:
  1.3 50.5 %shard_map.111 = (bf16[192,128]{1,0:T(8,128)(2,1)S(1)}, f32[192,128]{1,0:T(8,128)S(1)}, f32[192,128]{1,0:T(8,128)S(1)}, bf16[16,2,128,128]{3,2,1,0:T(8,128)(2,1)S(1)}) custom-call(s32[2,16]{1,0:T(2,128)} %bitcast.17, f32[1]{0:T(128)S(6)} %copy.16.coeff, bf16[16,2,128,128]{3,2,1,0:T(8,128)(2,1)} %h.1, bf16[192,128]{1,0:T(8,128)(2,1)} %bitcast.13, ...), custom_call_target="tpu_custom_call" | custom-call | flops 603979776 | bytes 2588672 | tf_op jit(solution)/shard_map/pallas_call | solution.py:409
  51.8 0.6 %copy.17 = bf16[128,192]{0,1:T(8,128)(2,1)} copy(bf16[128,192]{0,1:T(8,128)(2,1)S(1)} %bitcast.11) | data formatting | bytes 98304
  52.4 0.6 %copy.18 = f32[128,192]{0,1:T(8,128)} copy(f32[128,192]{0,1:T(8,128)S(1)} %bitcast.10) | data formatting | bytes 196608
  53.1 0.6 %copy.19 = f32[128,192]{0,1:T(8,128)} copy(f32[128,192]{0,1:T(8,128)S(1)} %bitcast.9) | data formatting | bytes 196608
  53.7 1.0 %copy.20 = bf16[16,2,128,128]{3,2,1,0:T(8,128)(2,1)} copy(bf16[16,2,128,128]{3,2,1,0:T(8,128)(2,1)S(1)} %get-tuple-element.19) | data formatting | bytes 2097152

commit v4 on v3

v4 whole, which is shorter than its diff:
```python
import functools

import jax
import jax.numpy as jnp
from jax import lax
from jax.experimental import pallas as pl
from jax.experimental.pallas import tpu as pltpu
from jax.sharding import PartitionSpec as P

MESH = pl.DeviceIdType.MESH
F32 = jnp.float32
BF16 = jnp.bfloat16
NT = (((1,), (1,)), ((), ()))
NN = (((1,), (0,)), ((), ()))
TN = (((0,), (0,)), ((), ()))


def dot(a, b, dims):
    return lax.dot_general(a, b, dims, preferred_element_type=F32)


def kernel(
    rows, inner, cols, coeff, h, now, prev, dens, cotp, cotd,
    o_next, o_dens, o_grad, o_gh,
    hbuf, v_prev, v_dens, v_cotp, v_cotd,
    win, cot, chain, tout, tsib, ysend, yrecv, pout, psib, rsend, rrecv,
    where, link, v_links,
    in_sem, ring_s, ring_r, sib_s, sib_r, y_s, y_r, ysib_s, ysib_r,
    tsib_s, tsib_r, ty_s, ty_r, psib_s, psib_r, rs_s, rs_r,
):
    zs = inner // 2
    half = zs // 2
    nv, bs = win.shape[1:]
    part = (pl.ds(0, nv // 2), pl.ds(nv // 2, nv // 2))
    pairs = 2 * inner
    total_blocks = rows * inner
    r = lax.axis_index("row")
    i = lax.axis_index("inner")
    z, c = i // 2, lax.rem(i, 2)
    o = 1 - c

    offs = [0]
    for k in range(1, half):
        offs += [-k, k]
    offs.append(half)

    def at_z(step):
        return lax.rem(z + step + zs, zs)

    sibling = (r, 2 * z + o)
    along = ((r, 2 * at_z(1) + c), (r, 2 * at_z(-1) + c))
    beyond = ((r, 2 * at_z(2) + c), (r, 2 * at_z(-2) + c))
    row_up = (lax.rem(r + 1, rows), i)
    row_down = (lax.rem(r + rows - 1, rows), i)
    started = []

    def send(src, dst, s, v, device):
        copy = pltpu.make_async_remote_copy(
            src_ref=src, dst_ref=dst, send_sem=s, recv_sem=v,
            device_id=device, device_id_type=MESH,
        )
        copy.start()
        started.append(copy)
        return copy

    def pos(g, parity, j=0):
        return (g * 2 + parity) * zs + j

    def run(g, parity, span):
        return pl.ds(pos(g, parity, span[0]), span[1])

    loads = []
    for k, (src, dst) in enumerate(
        ((now, win.at[pos(1, c)]), (cotp, v_cotp), (cotd, v_cotd), (h, hbuf), (prev, v_prev), (dens, v_dens))
    ):
        copy = pltpu.make_async_copy(src, dst, in_sem.at[k])
        copy.start()
        loads.append(copy)

    barrier = pltpu.get_barrier_semaphore()
    for device in (sibling, *along, *beyond, row_up, row_down):
        pl.semaphore_signal(barrier, inc=1, device_id=device, device_id_type=MESH)

    scale = coeff[0]
    loads[1].wait()
    loads[2].wait()
    cot[pos(0, c)] = (v_cotp[...].astype(F32) + scale * v_cotd[...].astype(F32)).astype(BF16)
    loads[0].wait()
    pl.semaphore_wait(barrier, 7)

    held = (win, cot)
    base = (1, 0)
    ring = {}
    sib = {}
    ysent = {}
    spans = [(0, 1)] + [(2 * k - 1, 2) for k in range(1, half)] + [(zs - 1, 1)]

    def place(a, j):
        return held[a].at[pos(base[a], c, j)]

    def pass_on(a, way, kind):
        came, goes, device = (
            (0, 3, beyond), (0, 1, along), (3, 5, along), (3, zs - 1, beyond)
        )[kind]
        src = place(a, came + way if came else 0)
        dst = place(a, goes + way if kind < 3 else goes)
        if kind == 3:
            src, dst = src.at[part[way]], dst.at[part[way]]
        ring[a, way, kind] = send(
            src, dst, ring_s.at[a, way, kind], ring_r.at[a, way, kind], device[way]
        )

    def own_out(a, kind):
        for way in range(2):
            pass_on(a, way, kind)

    def came_in(a, kind):
        for way in range(2):
            ring[a, way, kind].wait_recv()
            if kind == 0:
                pass_on(a, way, 2)
                pass_on(a, way, 3)

    def to_sibling(a, n):
        ref = held[a].at[run(base[a], c, spans[n])]
        sib[a, n] = send(ref, ref, sib_s.at[a, n], sib_r.at[a, n], sibling)

    def to_rows(n):
        src = win.at[run(1, c, spans[n])]
        for way, g, device in ((0, 2, row_down), (1, 0, row_up)):
            ysent[way, n] = send(
                src, win.at[run(g, c, spans[n])], y_s.at[way, n], y_r.at[way, n], device
            )

    own_out(1, 0)
    own_out(1, 1)
    to_sibling(1, 0)
    to_rows(0)
    own_out(0, 0)

    def block_of(j, parity):
        return 2 * at_z(offs[j]) + parity

    uses = []
    for n, whose in (
        (0, 0), (0, 1), (2, 0), (2, 1), (1, 0), (1, 1), (3, 0), (4, 0), (3, 1), (4, 1)
    ):
        begin, count = spans[n]
        uses += [(j, whose) for j in range(begin, begin + count)]
    parities = (c, o)

    first = r * inner
    listed = []
    for n, (j, whose) in enumerate(uses):
        b = block_of(j, parities[whose])
        for s in range(2):
            w = lax.rem(cols[s, b] - first + inner + total_blocks, total_blocks)
            w = jnp.minimum(w, 3 * inner - 1)
            g, ii = w // inner, lax.rem(w, inner)
            rel = lax.rem(ii // 2 - z + zs, zs)
            jj = jnp.where(rel <= half, jnp.minimum(2 * rel, zs - 1), 2 * (zs - rel) - 1)
            listed.append(pos(g, lax.rem(ii, 2), jj))
            where[2 * n + s] = listed[-1]

    lane = lax.broadcasted_iota(jnp.int32, (1, 128), 1)
    ends = jnp.full((1, 128), pairs, jnp.int32)
    spots = jnp.full((1, 128), -1, jnp.int32)
    before = jnp.full((1, 128), pairs, jnp.int32)
    for q in range(pairs):
        ends = jnp.where(lane == listed[q], q, ends)
        spots = jnp.where(lane == q, listed[q], spots)
    for q in range(pairs):
        before = jnp.where((spots == listed[q]) & (lane > q), q, before)
    v_links[0:1, :] = ends
    v_links[1:2, :] = before
    links = pltpu.make_async_copy(v_links, link, in_sem.at[6])
    links.start()

    chain[pairs] = jnp.zeros((nv, bs), F32)

    def hcat(b):
        return jnp.concatenate([hbuf[b, 0], hbuf[b, 1]], axis=1)

    def back(n, j, parity):
        got = dot(cot[pos(0, parity, j)], hcat(block_of(j, parity)), NN)
        for s in range(2):
            q = 2 * n + s
            chain[q] = got[:, s * bs : (s + 1) * bs] + chain[link[1, q]]

    def backs(n, whose):
        begin, count = spans[n]
        for j in range(begin, begin + count):
            back(uses.index((j, whose)), j, parities[whose])

    ysib = {}
    packs = ((0, half + 1), (half + 1, half - 1))

    def y_wait(n):
        for way in range(2):
            ysent[way, n].wait_recv()

    def pack_out(m):
        for way, g in ((0, 2), (1, 0)):
            ref = win.at[run(g, c, packs[m])]
            ysib[way, m] = send(ref, ref, ysib_s.at[way, m], ysib_r.at[way, m], sibling)
        ref = win.at[run(1, c, packs[m])]
        ysib[2, m] = send(ref, ref, ysib_s.at[2, m], ysib_r.at[2, m], sibling)

    def backs_there(n):
        sib[1, n].wait_recv()
        backs(n, 1)

    came_in(1, 0)
    to_sibling(1, 2)
    own_out(0, 1)
    loads[3].wait()
    links.wait()
    backs(0, 0)
    backs_there(0)
    came_in(1, 1)
    to_sibling(1, 1)
    backs(2, 0)
    came_in(0, 0)
    to_rows(2)
    backs_there(2)
    backs(1, 0)
    came_in(1, 2)
    to_sibling(1, 3)
    came_in(1, 3)
    to_sibling(1, 4)
    came_in(0, 1)
    to_rows(1)
    backs_there(1)
    backs(3, 0)
    backs(4, 0)
    came_in(0, 2)
    to_rows(3)
    came_in(0, 3)
    to_rows(4)
    backs_there(3)
    backs_there(4)

    def tail(g, parity, j):
        return chain[link[0, pos(g, parity, j)]]

    cuts = ((zs - 3, 3), (zs - 5, 2), (0, zs - 5))
    tsent = {}

    def tails_out(k, g, m):
        begin, count = cuts[m]
        for j in range(begin, begin + count):
            tout[k, j] = tail(g, o, j).astype(BF16)
        span = pl.ds(begin, count)
        tsent[k, m] = send(
            tout.at[k, span], tsib.at[k, span], tsib_s.at[k, m], tsib_r.at[k, m], sibling
        )

    for m in range(3):
        tails_out(0, 0, m)
        tails_out(1, 2, m)

    for n in (0, 2, 1):
        y_wait(n)
    pack_out(0)
    ty = {}

    def to_owners(n):
        begin, count = spans[n]
        for k, g, device in ((0, 0, row_down), (1, 2, row_up)):
            for j in range(begin, begin + count):
                ysend[k, j] = (tail(g, c, j) + tsib[k, j].astype(F32)).astype(BF16)
            span = pl.ds(begin, count)
            ty[k, n] = send(
                ysend.at[k, span], yrecv.at[k, span], ty_s.at[k, n], ty_r.at[k, n], device
            )

    ready = {half: 0, half - 2: 1, half - 3: 2}
    for n in range(half, -1, -1):
        if n in ready:
            tsent[0, ready[n]].wait_recv()
            tsent[1, ready[n]].wait_recv()
        to_owners(n)
    y_wait(3)
    y_wait(4)
    pack_out(1)
    for m in range(3):
        tails_out(2, 1, m)
    for m in range(2):
        for way in range(3):
            ysib[way, m].wait_recv()

    def picked(n):
        return jnp.concatenate([win[where[2 * n]], win[where[2 * n + 1]]], axis=1)

    def product(n, j, parity, k):
        pout[k, j] = dot(picked(n), hcat(block_of(j, parity)), NT).astype(BF16)

    psent = {}
    for m in range(3):
        begin, count = cuts[m]
        for j in range(begin, begin + count):
            product(uses.index((j, 1)), j, o, 1)
        span = pl.ds(begin, count)
        psent[m] = send(pout.at[1, span], psib.at[span], psib_s.at[m], psib_r.at[m], sibling)
    for j in range(zs - 1, -1, -1):
        product(uses.index((j, 0)), j, c, 0)

    def grad_rows(begin, count):
        for n in range(begin, begin + count):
            j, parity = uses[n][0], parities[uses[n][1]]
            b = block_of(j, parity)
            got = 2.0 * dot(cot[pos(0, parity, j)], picked(n), TN)
            for s in range(2):
                o_gh[b, s] = got[:, s * bs : (s + 1) * bs].astype(BF16)

    def product_here(j):
        return pout[0, j].astype(F32) + psib[j].astype(F32)

    def term_here(j):
        return (
            tail(1, c, j) + tsib[2, j].astype(F32)
            + yrecv[0, j].astype(F32) + yrecv[1, j].astype(F32)
        )

    here = (product_here, term_here)
    rs = {}

    def rs_send(a, way, kind, value, device, span=None):
        out, got = rsend.at[a, way, kind], rrecv.at[a, way, kind]
        if span is not None:
            out, got = out.at[span], got.at[span]
        out[...] = value.astype(BF16)
        rs[a, way, kind] = send(
            out, got, rs_s.at[a, way, kind], rs_r.at[a, way, kind], device[way]
        )

    def rs_far(a):
        far = here[a](zs - 1)
        for way in range(2):
            start = way * (nv // 2)
            rs_send(a, way, 1, far[start : start + nv // 2], beyond, part[way])
        for way in range(2):
            rs_send(a, way, 0, here[a](6 - way), along)

    def rs_middle(a):
        for way in range(2):
            value = here[a](4 - way)
            rs[a, way, 1].wait_recv()
            rs[a, way, 0].wait_recv()
            more = rrecv[a, way, 1, part[way], :].astype(F32)
            blank = jnp.zeros_like(more)
            more = jnp.concatenate((more, blank) if way == 0 else (blank, more), axis=0)
            value = value + rrecv[a, way, 0].astype(F32) + more
            rs_send(a, way, 2, value, beyond)

    def rs_near(a):
        for way in range(2):
            rs_send(a, way, 3, here[a](2 - way), along)

    def finish(a):
        value = here[a](0)
        for way in range(2):
            for kind in (3, 2):
                rs[a, way, kind].wait_recv()
                value = value + rrecv[a, way, kind].astype(F32)
        return value

    def y_here(n):
        for k in range(2):
            ty[k, n].wait_recv()

    chunk = inner // 4
    psent[0].wait_recv()
    rs_far(0)
    grad_rows(0, chunk)
    y_here(4)
    y_here(3)
    tsent[2, 0].wait_recv()
    rs_far(1)
    psent[1].wait_recv()
    rs_middle(0)
    psent[2].wait_recv()
    rs_near(0)
    grad_rows(chunk, chunk)
    y_here(2)
    tsent[2, 1].wait_recv()
    rs_middle(1)
    y_here(1)
    tsent[2, 2].wait_recv()
    rs_near(1)
    grad_rows(2 * chunk, 2 * chunk)

    loads[4].wait()
    loads[5].wait()
    nxt = (2.0 * finish(0) - v_prev[...].astype(F32)).astype(BF16)
    o_next[...] = nxt
    o_dens[...] = v_dens[...] + scale * nxt.astype(F32)
    y_here(0)
    o_grad[...] = 2.0 * finish(1)
    for copy in started:
        copy.wait_send()


def write_out(*refs):
    count = len(refs) // 2
    sems = refs[-1]
    copies = [
        pltpu.make_async_copy(refs[k], refs[count + k], sems.at[k]) for k in range(count)
    ]
    for copy in copies:
        copy.start()
    for copy in copies:
        copy.wait()


def per_device(h, cols, now, prev, dens, coeff, cotp, cotd):
    inner, slots, bs, _ = h.shape
    nv = now.shape[1]
    rows = lax.axis_size("row")
    zs, half = inner // 2, inner // 4
    pairs = inner * slots
    blk = (nv, bs)
    any_spec = pl.BlockSpec(memory_space=pl.ANY)
    hbm = pl.BlockSpec(memory_space=pltpu.HBM)
    vmem = pl.BlockSpec(memory_space=pltpu.VMEM)
    smem = pl.BlockSpec(memory_space=pltpu.SMEM)
    vm = pltpu.VMEM
    sem = lambda *shape: pltpu.SemaphoreType.DMA(shape)
    scratch = [
        vm(h.shape, BF16),
        vm(blk, BF16), vm(blk, F32), vm(blk, BF16), vm(blk, BF16),
        vm((3 * inner, *blk), BF16), vm((inner, *blk), BF16), vm((pairs + 1, *blk), F32),
        vm((3, zs, *blk), BF16), vm((3, zs, *blk), BF16),
        vm((2, zs, *blk), BF16), vm((2, zs, *blk), BF16),
        vm((2, zs, *blk), BF16), vm((zs, *blk), BF16),
        vm((2, 2, half, *blk), BF16), vm((2, 2, half, *blk), BF16),
        pltpu.SMEM((pairs,), jnp.int32), pltpu.SMEM((2, 128), jnp.int32),
        vm((2, 128), jnp.int32),
        sem(7), sem(2, 2, 4), sem(2, 2, 4), sem(2, half + 1), sem(2, half + 1),
        sem(2, half + 1), sem(2, half + 1), sem(3, 2), sem(3, 2),
        sem(3, 3), sem(3, 3), sem(2, half + 1), sem(2, half + 1), sem(3), sem(3),
        sem(2, 2, 4), sem(2, 2, 4),
    ]
    out = pl.pallas_call(
        functools.partial(kernel, rows, inner),
        out_shape=(
            jax.ShapeDtypeStruct(blk, BF16),
            jax.ShapeDtypeStruct(blk, F32),
            jax.ShapeDtypeStruct(blk, F32),
            jax.ShapeDtypeStruct(h.shape, BF16),
        ),
        in_specs=[smem, smem] + [hbm] * 6,
        out_specs=(vmem,) * 4,
        scratch_shapes=scratch,
        compiler_params=pltpu.CompilerParams(
            collective_id=0, has_side_effects=True, vmem_limit_bytes=40 * 1024 * 1024
        ),
        cost_estimate=pl.CostEstimate(
            flops=6 * pairs * bs * bs * nv, bytes_accessed=4 * h.size + 20 * bs * nv, transcendentals=0
        ),
    )(pltpu.with_memory_space_constraint(cols.T, pltpu.HBM), coeff, *[pltpu.with_memory_space_constraint(x, pltpu.HBM) for x in (h, now.T, prev.T, dens.T, cotp.T, cotd.T)])
    out = pl.pallas_call(
        write_out,
        out_shape=tuple(jax.ShapeDtypeStruct(x.shape, x.dtype) for x in out),
        in_specs=[any_spec] * 4,
        out_specs=(any_spec,) * 4,
        scratch_shapes=[sem(4)],
        compiler_params=pltpu.CompilerParams(vmem_limit_bytes=1024 * 1024),
    )(*out)
    return (out[0].T, out[1].T, out[2].T, out[3])


def solution(mesh):
    both = P(("row", "inner"), None)
    blocks = P("row", "inner", None, None)
    return jax.shard_map(
        per_device,
        mesh=mesh,
        in_specs=(blocks, P("row", "inner"), both, both, both, P(), both, both),
        out_specs=(both, both, both, blocks),
        check_vma=False,
    )
```

time: 54.8 us -> 53.2 us (0.971)
  local copies, waits for them, and re-layouts: 2.87 us -> 0 us
  Pallas kernels: 50.5 us -> 51.7 us
    unnamed x4 -> x0, local copies, waits for them, and re-layouts: 2.87 us -> none
    pallas_call x0 -> x1, Pallas kernels: none -> 1.09 us  [per_device(): pl.pallas_call(write_out, out_shape=tuple((jax.ShapeDtypeStruct(x.shape,...]
where the time goes in v4:
time: 53.2 us; the launch traced here: 53 us
  Pallas kernels  51.7 us (97%)
  between operations  1.29 us (2%)
    pallas_call x1, Pallas kernels, per_device(): pl.pallas_call(functools.partial(kernel, rows, inner), out_shape=(jax.Sha...  50.6 us
    pallas_call x1, Pallas kernels, per_device(): pl.pallas_call(write_out, out_shape=tuple((jax.ShapeDtypeStruct(x.shape,...  1.09 us

profile of v4, /device:TPU:1, one launch (start us, length us, event | category | flops | bytes accessed | tf_op | source)
XLA Modules:
  0.0 53.0 jit_solution(5891495442168771297)
XLA Ops:
  1.3 50.6 %shard_map.111 = (bf16[192,128]{1,0:T(8,128)(2,1)S(1)}, f32[192,128]{1,0:T(8,128)S(1)}, f32[192,128]{1,0:T(8,128)S(1)}, bf16[16,2,128,128]{3,2,1,0:T(8,128)(2,1)S(1)}) custom-call(s32[2,16]{1,0:T(2,128)} %bitcast.17, f32[1]{0:T(128)S(6)} %copy.12.coeff, bf16[16,2,128,128]{3,2,1,0:T(8,128)(2,1)} %h.1, bf16[192,128]{1,0:T(8,128)(2,1)} %bitcast.12, ...), custom_call_target="tpu_custom_call" | custom-call | flops 603979776 | bytes 2588672 | tf_op jit(solution)/shard_map/pallas_call | solution.py:444
  51.9 1.1 %shard_map.112 = (bf16[192,128]{1,0:T(8,128)(2,1)}, f32[192,128]{1,0:T(8,128)}, f32[192,128]{1,0:T(8,128)}, bf16[16,2,128,128]{3,2,1,0:T(8,128)(2,1)}) custom-call(bf16[192,128]{1,0:T(8,128)(2,1)S(1)} %get-tuple-element.12.refs_0_, f32[192,128]{1,0:T(8,128)S(1)} %get-tuple-element.13.refs_1_, f32[192,128]{1,0:T(8,128)S(1)} %get-tuple-element.14.refs_2_, ...), custom_call_target="tpu_custom_call" | custom-call | tf_op jit(solution)/shard_map/pallas_call | solution.py:462

commit v5 on v4

--- a/solution.py
+++ b/solution.py
@@ -262,6 +262,9 @@
     for n in (0, 2, 1):
         y_wait(n)
     pack_out(0)
+    y_wait(3)
+    y_wait(4)
+    pack_out(1)
     ty = {}
 
     def to_owners(n):
@@ -280,9 +283,6 @@
             tsent[0, ready[n]].wait_recv()
             tsent[1, ready[n]].wait_recv()
         to_owners(n)
-    y_wait(3)
-    y_wait(4)
-    pack_out(1)
     for m in range(3):
         tails_out(2, 1, m)
     for m in range(2):
@@ -372,6 +372,8 @@
     chunk = inner // 4
     psent[0].wait_recv()
     rs_far(0)
+    psent[2].wait_recv()
+    rs_near(0)
     grad_rows(0, chunk)
     y_here(4)
     y_here(3)
@@ -379,8 +381,6 @@
     rs_far(1)
     psent[1].wait_recv()
     rs_middle(0)
-    psent[2].wait_recv()
-    rs_near(0)
     grad_rows(chunk, chunk)
     y_here(2)
     tsent[2, 1].wait_recv()

time: 53.2 us -> 52.6 us (0.989)
    pallas_call x1, Pallas kernels: 50.6 us -> 50.1 us  [per_device(): pl.pallas_call(functools.partial(kernel, rows, inner), out_shape=(jax.Sha...]
where the time goes in v5:
time: 52.6 us; the launch traced here: 52.5 us
  Pallas kernels  51.2 us (97%)
  between operations  1.29 us (2%)
    pallas_call x1, Pallas kernels, per_device(): pl.pallas_call(functools.partial(kernel, rows, inner), out_shape=(jax.Sha...  50.1 us
    pallas_call x1, Pallas kernels, per_device(): pl.pallas_call(write_out, out_shape=tuple((jax.ShapeDtypeStruct(x.shape,...  1.09 us

profile of v5, /device:TPU:1, one launch (start us, length us, event | category | flops | bytes accessed | tf_op | source)
XLA Modules:
  0.0 52.5 jit_solution(11107854853274500354)
XLA Ops:
  1.3 50.1 %shard_map.111 = (bf16[192,128]{1,0:T(8,128)(2,1)S(1)}, f32[192,128]{1,0:T(8,128)S(1)}, f32[192,128]{1,0:T(8,128)S(1)}, bf16[16,2,128,128]{3,2,1,0:T(8,128)(2,1)S(1)}) custom-call(s32[2,16]{1,0:T(2,128)} %bitcast.17, f32[1]{0:T(128)S(6)} %copy.12.coeff, bf16[16,2,128,128]{3,2,1,0:T(8,128)(2,1)} %h.1, bf16[192,128]{1,0:T(8,128)(2,1)} %bitcast.12, ...), custom_call_target="tpu_custom_call" | custom-call | flops 603979776 | bytes 2588672 | tf_op jit(solution)/shard_map/pallas_call | solution.py:444
  51.4 1.1 %shard_map.112 = (bf16[192,128]{1,0:T(8,128)(2,1)}, f32[192,128]{1,0:T(8,128)}, f32[192,128]{1,0:T(8,128)}, bf16[16,2,128,128]{3,2,1,0:T(8,128)(2,1)}) custom-call(bf16[192,128]{1,0:T(8,128)(2,1)S(1)} %get-tuple-element.12.refs_0_, f32[192,128]{1,0:T(8,128)S(1)} %get-tuple-element.13.refs_1_, f32[192,128]{1,0:T(8,128)S(1)} %get-tuple-element.14.refs_2_, ...), custom_call_target="tpu_custom_call" | custom-call | tf_op jit(solution)/shard_map/pallas_call | solution.py:462

commit v6 on v5

--- a/solution.py
+++ b/solution.py
@@ -136,6 +136,7 @@
     own_out(1, 1)
     to_sibling(1, 0)
     to_rows(0)
+    own_out(0, 1)
     own_out(0, 0)
 
     def block_of(j, parity):
@@ -212,7 +213,6 @@
 
     came_in(1, 0)
     to_sibling(1, 2)
-    own_out(0, 1)
     loads[3].wait()
     links.wait()
     backs(0, 0)
@@ -220,6 +220,8 @@
     came_in(1, 1)
     to_sibling(1, 1)
     backs(2, 0)
+    came_in(0, 1)
+    to_rows(1)
     came_in(0, 0)
     to_rows(2)
     backs_there(2)
@@ -228,8 +230,6 @@
     to_sibling(1, 3)
     came_in(1, 3)
     to_sibling(1, 4)
-    came_in(0, 1)
-    to_rows(1)
     backs_there(1)
     backs(3, 0)
     backs(4, 0)

time: 52.6 us -> 52.2 us (level)
  no operation moved by 1% of the time
where the time goes in v6:
time: 52.2 us; the launch traced here: 52 us
  Pallas kernels  50.7 us (97%)
  between operations  1.29 us (2%)
    pallas_call x1, Pallas kernels, per_device(): pl.pallas_call(functools.partial(kernel, rows, inner), out_shape=(jax.Sha...  49.6 us
    pallas_call x1, Pallas kernels, per_device(): pl.pallas_call(write_out, out_shape=tuple((jax.ShapeDtypeStruct(x.shape,...  1.09 us

profile of v6, /device:TPU:1, one launch (start us, length us, event | category | flops | bytes accessed | tf_op | source)
XLA Modules:
  0.0 52.0 jit_solution(12095801146865691864)
XLA Ops:
  1.3 49.6 %shard_map.111 = (bf16[192,128]{1,0:T(8,128)(2,1)S(1)}, f32[192,128]{1,0:T(8,128)S(1)}, f32[192,128]{1,0:T(8,128)S(1)}, bf16[16,2,128,128]{3,2,1,0:T(8,128)(2,1)S(1)}) custom-call(s32[2,16]{1,0:T(2,128)} %bitcast.17, f32[1]{0:T(128)S(6)} %copy.12.coeff, bf16[16,2,128,128]{3,2,1,0:T(8,128)(2,1)} %h.1, bf16[192,128]{1,0:T(8,128)(2,1)} %bitcast.12, ...), custom_call_target="tpu_custom_call" | custom-call | flops 603979776 | bytes 2588672 | tf_op jit(solution)/shard_map/pallas_call | solution.py:444
  50.9 1.1 %shard_map.112 = (bf16[192,128]{1,0:T(8,128)(2,1)}, f32[192,128]{1,0:T(8,128)}, f32[192,128]{1,0:T(8,128)}, bf16[16,2,128,128]{3,2,1,0:T(8,128)(2,1)}) custom-call(bf16[192,128]{1,0:T(8,128)(2,1)S(1)} %get-tuple-element.12.refs_0_, f32[192,128]{1,0:T(8,128)S(1)} %get-tuple-element.13.refs_1_, f32[192,128]{1,0:T(8,128)S(1)} %get-tuple-element.14.refs_2_, ...), custom_call_target="tpu_custom_call" | custom-call | tf_op jit(solution)/shard_map/pallas_call | solution.py:462

commit v7 on v6

--- a/solution.py
+++ b/solution.py
@@ -132,10 +132,10 @@
                 src, win.at[run(g, c, spans[n])], y_s.at[way, n], y_r.at[way, n], device
             )
 
+    to_rows(0)
     own_out(1, 0)
     own_out(1, 1)
     to_sibling(1, 0)
-    to_rows(0)
     own_out(0, 1)
     own_out(0, 0)
 
@@ -374,11 +374,11 @@
     rs_far(0)
     psent[2].wait_recv()
     rs_near(0)
-    grad_rows(0, chunk)
     y_here(4)
     y_here(3)
     tsent[2, 0].wait_recv()
     rs_far(1)
+    grad_rows(0, chunk)
     psent[1].wait_recv()
     rs_middle(0)
     grad_rows(chunk, chunk)

time: 52.2 us -> 52.2 us (level)
  no operation moved by 1% of the time
where the time goes in v7:
time: 52.2 us; the launch traced here: 52 us
  Pallas kernels  50.7 us (97%)
  between operations  1.29 us (2%)
    pallas_call x1, Pallas kernels, per_device(): pl.pallas_call(functools.partial(kernel, rows, inner), out_shape=(jax.Sha...  49.6 us
    pallas_call x1, Pallas kernels, per_device(): pl.pallas_call(write_out, out_shape=tuple((jax.ShapeDtypeStruct(x.shape,...  1.09 us

profile of v7, /device:TPU:1, one launch (start us, length us, event | category | flops | bytes accessed | tf_op | source)
XLA Modules:
  0.0 52.0 jit_solution(17516643622459001922)
XLA Ops:
  1.3 49.6 %shard_map.111 = (bf16[192,128]{1,0:T(8,128)(2,1)S(1)}, f32[192,128]{1,0:T(8,128)S(1)}, f32[192,128]{1,0:T(8,128)S(1)}, bf16[16,2,128,128]{3,2,1,0:T(8,128)(2,1)S(1)}) custom-call(s32[2,16]{1,0:T(2,128)} %bitcast.17, f32[1]{0:T(128)S(6)} %copy.12.coeff, bf16[16,2,128,128]{3,2,1,0:T(8,128)(2,1)} %h.1, bf16[192,128]{1,0:T(8,128)(2,1)} %bitcast.12, ...), custom_call_target="tpu_custom_call" | custom-call | flops 603979776 | bytes 2588672 | tf_op jit(solution)/shard_map/pallas_call | solution.py:444
  50.9 1.1 %shard_map.112 = (bf16[192,128]{1,0:T(8,128)(2,1)}, f32[192,128]{1,0:T(8,128)}, f32[192,128]{1,0:T(8,128)}, bf16[16,2,128,128]{3,2,1,0:T(8,128)(2,1)}) custom-call(bf16[192,128]{1,0:T(8,128)(2,1)S(1)} %get-tuple-element.12.refs_0_, f32[192,128]{1,0:T(8,128)S(1)} %get-tuple-element.13.refs_1_, f32[192,128]{1,0:T(8,128)S(1)} %get-tuple-element.14.refs_2_, ...), custom_call_target="tpu_custom_call" | custom-call | tf_op jit(solution)/shard_map/pallas_call | solution.py:462
